TPU v7x, 32 devices: a whole 2x2x4 slice. The times are simulated.
32 devices in a mesh: grp: 2 (over y), pool: 4 (over z), head: 2 (over x), aux: 2 (over core).
Axes of the slice: x: 2, y: 2, z: 4, core: 2. Of those that a mesh axis runs over, the one named last changes fastest.
Arguments:
- hidden: bfloat16 [16, 8192], P('grp', ('pool', 'head', 'aux')), parts along dimension 0, may hold values from -0.59765625 to 0.59765625
- gain: float32 [8192], P(('pool', 'head', 'aux')), may hold values from 0.5 to 1.5
- queries: bfloat16 [16, 8192], P(('grp', 'pool'), 'aux'), parts along dimension 0, may hold values from -6 to 6
- new_key: bfloat16 [16, 1024], P(('grp', 'pool'), 'aux'), parts along dimension 0, may hold values from -6 to 6
- new_value: bfloat16 [16, 1024], P(('grp', 'pool'), 'aux'), parts along dimension 0, may hold values from -6 to 6
- cache_key: bfloat16 [16, 512, 1024], P(('grp', 'pool'), 'head', 'aux'), parts along dimension 0, may hold values from -6 to 6
- cache_value: bfloat16 [16, 512, 1024], P(('grp', 'pool'), 'head', 'aux'), parts along dimension 0, may hold values from -6 to 6
- lengths: int32 [16], P('grp'), parts along dimension 0, may hold values from 170 to 512, as said below
- slot_of: int32 [16], P('grp'), parts along dimension 0, may hold values from 0 to 7, as said below
- out_proj: bfloat16 [2, 4096, 8192], P('aux', 'head', 'pool'), may hold values from -0.09375 to 0.09375
- lm_head: bfloat16 [8192, 65536], P(None, ('pool', 'head', 'aux')), may hold values from -1 to 1
Outputs:
- logits: float32 [16, 65536], P('grp', ('pool', 'head', 'aux')), parts along dimension 0
- entropy: float32 [16], P('grp'), parts along dimension 0
There are 2 independent parts, one for each index of `grp`. A program takes and returns all parts, laid end to end along the dimension named above; an argument that names none is the same for every part. Nothing has to cross between parts.
Inputs may be any that keep to these rules, and one draw needn't show every extreme that they name: `lengths`: some request fills all 512 positions and some has exactly 170. `slot_of`: each slot holds exactly one request; the requests of one index of pool have their slots together on one index of pool.
All inputs are finite; a program needn't handle non-finite values.
Results may differ from a plain program's by a relative error of at most 0.02.
Values may be sent and summed in bfloat16 or wider, within the bound.
A program may use at most 128 MiB of HBM per device.

v0:
```python
import math

import jax
import jax.numpy as jnp
from jax import lax
from jax.sharding import PartitionSpec as P

HD = 128


def select_rows(onehot, rows):
    return jnp.dot(onehot.astype(jnp.bfloat16), rows, preferred_element_type=jnp.float32).astype(
        jnp.bfloat16
    )


def per_device(
    hidden,
    gain,
    queries,
    new_key,
    new_value,
    cache_key,
    cache_value,
    lengths,
    slot_of,
    out_proj,
    lm_head,
):
    slots_here = cache_key.shape[0]
    span = cache_key.shape[1]
    kv_here = cache_key.shape[2] // HD
    q_here = queries.shape[1] // HD
    group = q_here // kv_here
    heads_out = out_proj.shape[1] // HD
    scale = 1.0 / math.sqrt(HD)
    pool_place = lax.axis_index("pool")
    head_place = lax.axis_index("head")
    all_queries, all_keys, all_values = (
        lax.all_gather(queries, "pool", axis=0, tiled=True),
        lax.all_gather(new_key, "pool", axis=0, tiled=True),
        lax.all_gather(new_value, "pool", axis=0, tiled=True),
    )
    requests = all_queries.shape[0]
    slot_ids = pool_place * slots_here + jnp.arange(slots_here, dtype=jnp.int32)
    chosen = slot_of[None, :] == slot_ids[:, None]
    query_slot = select_rows(chosen, all_queries)
    key_slot = select_rows(chosen, all_keys)
    value_slot = select_rows(chosen, all_values)
    length_slot = jnp.sum(jnp.where(chosen, lengths[None, :], 0), axis=1)
    query_heads = query_slot.reshape(slots_here, kv_here, group, HD)
    keys = cache_key.reshape(slots_here, span, kv_here, HD)
    values = cache_value.reshape(slots_here, span, kv_here, HD)
    scores = (
        jnp.einsum("skgd,stkd->skgt", query_heads, keys, preferred_element_type=jnp.float32) * scale
    )
    position = head_place * span + jnp.arange(span, dtype=jnp.int32)
    live = position[None, :] < length_slot[:, None]
    weights = jnp.where(live[:, None, None, :], jnp.exp(scores), 0.0)
    total = jnp.sum(weights, axis=3).reshape(slots_here, q_here)
    mixed = jnp.einsum(
        "skgt,stkd->skgd", weights.astype(jnp.bfloat16), values, preferred_element_type=jnp.float32
    )
    mixed = mixed.reshape(slots_here, q_here * HD)
    total, mixed = (
        lax.psum(total.astype(jnp.bfloat16), "head").astype(jnp.float32),
        lax.psum(mixed.astype(jnp.bfloat16), "head").astype(jnp.float32),
    )
    total = lax.dynamic_slice_in_dim(total, head_place * heads_out, heads_out, 1)
    mixed = lax.dynamic_slice_in_dim(mixed, head_place * heads_out * HD, heads_out * HD, 1)
    query_own = lax.dynamic_slice_in_dim(query_slot, head_place * heads_out * HD, heads_out * HD, 1)
    query_own = query_own.reshape(slots_here, heads_out, HD).astype(jnp.float32)
    key_spread = jnp.repeat(key_slot.reshape(slots_here, kv_here, HD), group, axis=1)
    value_spread = jnp.repeat(value_slot.reshape(slots_here, kv_here, HD), group, axis=1)
    key_own = lax.dynamic_slice_in_dim(key_spread, head_place * heads_out, heads_out, 1).astype(
        jnp.float32
    )
    value_own = lax.dynamic_slice_in_dim(value_spread, head_place * heads_out, heads_out, 1).astype(
        jnp.float32
    )
    own = jnp.exp(jnp.sum(query_own * key_own, axis=2) * scale)
    total = total + own
    mixed = mixed.reshape(slots_here, heads_out, HD) + own[:, :, None] * value_own
    attended = (mixed / total[:, :, None]).astype(jnp.bfloat16).reshape(slots_here, heads_out * HD)
    outputs = lax.all_gather(attended, "pool", axis=0, tiled=True)
    order = slot_of[:, None] == jnp.arange(requests, dtype=jnp.int32)[None, :]
    by_request = select_rows(order, outputs)
    weight_block = out_proj[0]
    term = jnp.dot(by_request, weight_block, preferred_element_type=jnp.float32)
    projected = lax.psum(term.astype(jnp.bfloat16), ("head", "aux")).astype(jnp.float32)
    block_hidden, block_gain = (
        lax.all_gather(hidden, ("head", "aux"), axis=1, tiled=True),
        lax.all_gather(gain.astype(jnp.bfloat16), ("head", "aux"), axis=0, tiled=True).astype(
            gain.dtype
        ),
    )
    stream = (block_hidden.astype(jnp.float32) + projected).astype(jnp.bfloat16)
    full_stream, full_gain = (
        lax.all_gather(stream, "pool", axis=1, tiled=True),
        lax.all_gather(block_gain.astype(jnp.bfloat16), "pool", axis=0, tiled=True).astype(
            block_gain.dtype
        ),
    )
    stream_wide = full_stream.astype(jnp.float32)
    mean_sq = jnp.mean(stream_wide * stream_wide, axis=1, keepdims=True)
    normed = (stream_wide * lax.rsqrt(mean_sq + 1e-05) * full_gain[None, :]).astype(jnp.bfloat16)
    logits = jnp.dot(normed, lm_head, preferred_element_type=jnp.float32)
    expd = jnp.exp(logits)
    vocab_total, moment = lax.psum(
        (jnp.sum(expd, axis=1), jnp.sum(expd * logits, axis=1)), ("pool", "head", "aux")
    )
    entropy = jnp.log(vocab_total) - moment / vocab_total
    return (logits, entropy)


def solution(mesh):
    in_specs = (
        P("grp", ("pool", "head", "aux")),
        P(("pool", "head", "aux")),
        P(("grp", "pool"), "aux"),
        P(("grp", "pool"), "aux"),
        P(("grp", "pool"), "aux"),
        P(("grp", "pool"), "head", "aux"),
        P(("grp", "pool"), "head", "aux"),
        P("grp"),
        P("grp"),
        P("aux", "head", "pool"),
        P(None, ("pool", "head", "aux")),
    )
    out_specs = (P("grp", ("pool", "head", "aux")), P("grp"))
    return jax.shard_map(
        per_device, mesh=mesh, in_specs=in_specs, out_specs=out_specs, check_vma=False
    )
```

profile of v0, /device:TPU:0, one launch (start us, length us, event | category | flops | bytes accessed | tf_op | source)
XLA Modules:
  0.0 173.6 jit_solution(14851051543127274626)
XLA Ops:
  0.6 0.0 copy-start
  0.7 0.9 fusion.32
  1.6 0.1 broadcast_compare_fusion
  1.7 0.7 convert_element_type.99
  2.3 6.1 %all-gather.4 = bf16[4,1,512]{2,1,0:T(2,128)(2,1)S(1)} all-gather(bf16[1,1,512]{2,1,0:T(2,128)(2,1)S(1)} %reshape.104), channel_id=1, replica_groups=mesh['grp'=2,'pool'=4,'head'=2,'aux'=2] {'head','aux'}, dimensions={0}, use_global_device_ids=true | all-gather | bytes 5120 | tf_op jit(solution)/shard_map/all_gather | solution.py:93
  8.5 12.7 %all-gather.1 = bf16[4,2,512]{2,1,0:T(2,128)(2,1)S(1)} all-gather(bf16[1,2,512]{2,1,0:T(2,128)(2,1)} %bitcast.68), channel_id=1, replica_groups=mesh['grp'=2,'pool'=4,'head'=2,'aux'=2] {'pool'}, dimensions={0}, use_global_device_ids=true | all-gather | bytes 10240 | tf_op jit(solution)/shard_map/all_gather | solution.py:41
  21.2 0.8 convolution_convert_fusion.4
  22.1 12.0 %all-gather.2 = bf16[4,2,512]{2,1,0:T(2,128)(2,1)S(1)} all-gather(bf16[1,2,512]{2,1,0:T(2,128)(2,1)} %bitcast.69), channel_id=1, replica_groups=mesh['grp'=2,'pool'=4,'head'=2,'aux'=2] {'pool'}, dimensions={0}, use_global_device_ids=true | all-gather | bytes 10240 | tf_op jit(solution)/shard_map/all_gather | solution.py:42
  34.1 0.8 convolution_convert_fusion.3
  35.0 13.1 %all_gather.31 = bf16[8192]{0:T(1024)(128)(2,1)S(1)} all-gather(bf16[2048]{0:T(1024)(128)(2,1)S(1)} %bitcast.65), channel_id=1, replica_groups=mesh['grp'=2,'pool'=4,'head'=2,'aux'=2] {'pool'}, dimensions={0}, use_global_device_ids=true | all-gather | bytes 20480 | tf_op jit(solution)/shard_map/all_gather | solution.py:100
  48.1 5.4 %all_gather.24 = bf16[8,2048]{1,0:T(8,128)(2,1)S(1)} all-gather(bf16[8,512]{1,0:T(8,128)(2,1)} %param.11), channel_id=1, replica_groups=mesh['grp'=2,'pool'=4,'head'=2,'aux'=2] {'head','aux'}, dimensions={1}, use_global_device_ids=true | all-gather | bytes 40960 | tf_op jit(solution)/shard_map/all_gather | solution.py:92
  53.5 13.5 %all-gather = bf16[4,2,4096]{2,1,0:T(2,128)(2,1)S(1)} all-gather(bf16[1,2,4096]{2,1,0:T(2,128)(2,1)} %bitcast.64), channel_id=1, replica_groups=mesh['grp'=2,'pool'=4,'head'=2,'aux'=2] {'pool'}, dimensions={0}, use_global_device_ids=true | all-gather | bytes 81920 | tf_op jit(solution)/shard_map/all_gather | solution.py:40
  67.0 0.9 convolution_convert_fusion
  67.9 0.1 fusion.21
  68.0 0.0 copy-done
  68.0 0.3 fusion.39
  68.3 0.1 convert_element_type.91
  68.4 1.2 fusion.7
  69.7 8.3 %all-reduce.1 = (bf16[2,4096]{1,0:T(2,128)(2,1)S(1)}, bf16[2,32]{1,0:T(2,128)(2,1)S(1)}) all-reduce(bf16[2,4096]{1,0:T(2,128)(2,1)S(1)} %bitcast.63, bf16[2,32]{1,0:T(2,128)(2,1)S(1)} %convert_element_type.91), channel_id=1, replica_groups=mesh['grp'=2,'pool'=4,'head'=2,'aux'=2] {'head'}, use_global_device_ids=true, to_apply=%region_1.2 | all-reduce | flops 8256 | bytes 33024 | tf_op jit(solution)/shard_map/psum | solution.py:67
  77.9 0.1 multiply_exponential_fusion
  78.0 0.1 fusion.23
  78.1 13.1 %all-gather.3 = bf16[4,2,2048]{2,1,0:T(2,128)(2,1)S(1)} all-gather(bf16[1,2,2048]{2,1,0:T(2,128)(2,1)S(1)} %reshape.102), channel_id=1, replica_groups=mesh['grp'=2,'pool'=4,'head'=2,'aux'=2] {'pool'}, dimensions={0}, use_global_device_ids=true | all-gather | bytes 40960 | tf_op jit(solution)/shard_map/all_gather | solution.py:85
  91.3 4.7 %fusion.2 = bf16[8,2048]{1,0:T(8,128)(2,1)S(1)} fusion(bf16[1,2048,2048]{2,1,0:T(8,128)(2,1)} %param.20, bf16[8,2048]{1,0:T(8,128)(2,1)S(1)} %reshape.103, s32[8]{0:T(128)} %param.19), kind=kOutput, calls=%fused_computation.3 | convolution fusion | flops 67403840 | bytes 8454176 | tf_op jit(solution)/shard_map/dot_general | solution.py:89
  96.0 10.4 %psum.37 = bf16[8,2048]{1,0:T(8,128)(2,1)S(1)} all-reduce(bf16[8,2048]{1,0:T(8,128)(2,1)S(1)} %fusion.2), channel_id=1, replica_groups=mesh['grp'=2,'pool'=4,'head'=2,'aux'=2] {'head','aux'}, use_global_device_ids=true, to_apply=%region_5.6 | all-reduce | flops 16384 | bytes 65536 | tf_op jit(solution)/shard_map/psum | solution.py:90
  106.4 13.5 %all_gather.29 = bf16[8,8192]{1,0:T(8,128)(2,1)S(1)} all-gather(bf16[8,2048]{1,0:T(8,128)(2,1)S(1)} %add_convert_fusion), channel_id=1, replica_groups=mesh['grp'=2,'pool'=4,'head'=2,'aux'=2] {'pool'}, dimensions={1}, use_global_device_ids=true | all-gather | bytes 163840 | tf_op jit(solution)/shard_map/all_gather | solution.py:99
  119.9 0.2 fusion.12
  120.1 23.5 %exponential_reduce_fusion = (f32[8]{0:T(128)S(1)}, f32[8]{0:T(128)S(1)}, f32[8,4096]{1,0:T(8,128)}) fusion(bf16[8192,4096]{1,0:T(8,128)(2,1)} %param.21, bf16[8,8192]{1,0:T(8,128)(2,1)S(1)} %all_gather.29, f32[8192]{0:T(1024)S(1)} %convert_element_type.100, f32[8]{0:T(128)S(1)} %add_rsqrt_fusion), kind=kOutput, calls=%fused_computation.22 | convolution fusion | flops 537231360 | bytes 67403872 | tf_op jit(solution)/shard_map/dot_general | solution.py:107
  143.6 29.5 %all-reduce = (f32[8]{0:T(128)S(1)}, f32[8]{0:T(128)S(1)}) all-reduce(f32[8]{0:T(128)S(1)} %get-tuple-element.3, f32[8]{0:T(128)S(1)} %get-tuple-element.2), channel_id=1, replica_groups=mesh['grp'=2,'pool'=4,'head'=2,'aux'=2] {'pool','head','aux'}, use_global_device_ids=true, to_apply=%region_10.11 | all-reduce | flops 16 | bytes 128 | tf_op jit(solution)/shard_map/psum | solution.py:109
  173.1 0.5 divide_subtract_fusion
  (21 shorter events, 0.3 us)
Async XLA Ops:
  0.6 67.3 %copy-start = (bf16[2,256,512]{2,1,0:T(8,128)(2,1)S(1)}, bf16[2,256,512]{2,1,0:T(8,128)(2,1)}, u32[]{:S(2)}) copy-start(bf16[2,256,512]{2,1,0:T(8,128)(2,1)} %param.16) | copy-start | bytes 1572868
where the time goes:
time: 174 us
  blocking collectives  138 us (79%)
  matrix products  32.3 us (19%)
  other arithmetic  2.71 us (2%)
    psum x1, blocking collectives, per_device(): lax.psum((jnp.sum(expd, axis=1), jnp.sum(expd * logits, axis=1)), ('pool'...  29.5 us
    dot_general x1, matrix products, per_device(): logits = jnp.dot(normed, lm_head, preferred_element_type=jnp.float32)  23.5 us
    all_gather x1, blocking collectives, per_device(): lax.all_gather(stream, 'pool', axis=1, tiled=True)  13.5 us
    all_gather x1, blocking collectives, per_device(): lax.all_gather(queries, 'pool', axis=0, tiled=True)  13.5 us
    all_gather x1, blocking collectives, per_device(): outputs = lax.all_gather(attended, 'pool', axis=0, tiled=True)  13.1 us
    all_gather x1, blocking collectives, per_device(): lax.all_gather(block_gain.astype(jnp.bfloat16), 'pool', axis=0, tiled=True)  13.1 us
    all_gather x1, blocking collectives, per_device(): lax.all_gather(new_key, 'pool', axis=0, tiled=True)  12.7 us
    all_gather x1, blocking collectives, per_device(): lax.all_gather(new_value, 'pool', axis=0, tiled=True)  12 us

commit v1 on v0

--- a/solution.py
+++ b/solution.py
@@ -1,11 +1,495 @@
+import functools
 import math
 
 import jax
 import jax.numpy as jnp
 from jax import lax
+from jax.experimental import pallas as pl
+from jax.experimental.pallas import tpu as pltpu
 from jax.sharding import PartitionSpec as P
 
 HD = 128
+MESH = pl.DeviceIdType.MESH
+BF = jnp.bfloat16
+F32 = jnp.float32
+MIB = 1024 * 1024
+RING = 15
+
+
+def iota(shape, axis):
+    return lax.broadcasted_iota(jnp.int32, shape, axis)
+
+
+def mm(a, b):
+    return jnp.dot(a, b, preferred_element_type=F32)
+
+
+def pick(position, scalars):
+    out = jnp.full(position.shape, scalars[0], jnp.int32)
+    for r in range(1, len(scalars)):
+        out = jnp.where(position == r, scalars[r], out)
+    return out
+
+
+def kernel(
+    cfg,
+    slot_ref,
+    len_ref,
+    hidden_hbm,
+    gain_hbm,
+    q_hbm,
+    nk_hbm,
+    nv_hbm,
+    ck_hbm,
+    cv_hbm,
+    wo_hbm,
+    lm_hbm,
+    logits_hbm,
+    ent_ref,
+    ring,
+    ck,
+    cv,
+    qv,
+    nkv,
+    nvv,
+    hid,
+    gains,
+    stage,
+    xq,
+    send2,
+    recv2,
+    send3,
+    recv3,
+    xs,
+    acc,
+    xe,
+    ring_sem,
+    wo_sem,
+    in_sem,
+    out_sem,
+    q_send,
+    q_recv,
+    g_send,
+    g_recv,
+    a_send,
+    a_recv,
+    t_send,
+    t_recv,
+    s_send,
+    s_recv,
+    e_send,
+    e_recv,
+):
+    NP, NH, NA = cfg["NP"], cfg["NH"], cfg["NA"]
+    R, S, KV, G, SPAN = cfg["R"], cfg["S"], cfg["KV"], cfg["G"], cfg["SPAN"]
+    W, NCH, NBUF = cfg["W"], cfg["NCH"], cfg["NBUF"]
+    QL = KV * G
+    HO = QL // NH
+    QUAD = NH * NA
+    scale = 1.0 / math.sqrt(HD)
+    p = lax.axis_index("pool")
+    h = lax.axis_index("head")
+    a = lax.axis_index("aux")
+    me = (p * NH + h) * NA + a
+    everyone = [
+        (dp, dh, da)
+        for dp in range(NP)
+        for dh in range(NH)
+        for da in range(NA)
+        if (dp, dh, da) != (0, 0, 0)
+    ]
+
+    def at(dp, dh, da):
+        return {
+            "pool": lax.rem(p + dp, NP),
+            "head": lax.rem(h + dh, NH),
+            "aux": lax.rem(a + da, NA),
+        }
+
+    def place(where):
+        return (where["pool"] * NH + where["head"]) * NA + where["aux"]
+
+    barrier = pltpu.get_barrier_semaphore()
+    for d in everyone:
+        pl.semaphore_signal(barrier, inc=1, device_id=at(*d), device_id_type=MESH)
+
+    ins = [
+        pltpu.make_async_copy(src, dst, in_sem.at[i])
+        for i, (src, dst) in enumerate(
+            [
+                (q_hbm, qv),
+                (nk_hbm, nkv),
+                (nv_hbm, nvv),
+                (gain_hbm, gains.at[me]),
+                (hidden_hbm, hid),
+                (ck_hbm, ck),
+                (cv_hbm, cv),
+            ]
+        )
+    ]
+    for c in ins:
+        c.start()
+
+    DB = wo_hbm.shape[2]
+    ROWS, VL = ring.shape[1], ring.shape[2]
+    per = VL // DB
+    KO = wo_hbm.shape[1]
+    pieces = KO // ROWS
+    held_slots = pieces // per
+    wo_places = [
+        (NBUF - held_slots + i // per, (i % per) * DB, i * ROWS) for i in range(pieces)
+    ]
+    wo_copies = [
+        pltpu.make_async_copy(
+            wo_hbm.at[0, pl.ds(row, ROWS), :],
+            ring.at[slot, :, pl.ds(lane, DB)],
+            wo_sem.at[i],
+        )
+        for i, (slot, lane, row) in enumerate(wo_places)
+    ]
+    for c in wo_copies:
+        c.start()
+
+    def block_of(o):
+        return lax.rem(p * QUAD + o, NCH)
+
+    def lm_copy(o, slot):
+        row = pl.multiple_of(block_of(o) * ROWS, ROWS)
+        return pltpu.make_async_copy(
+            lm_hbm.at[pl.ds(row, ROWS), :], ring.at[slot], ring_sem.at[slot]
+        )
+
+    for o in range(NBUF - held_slots):
+        lm_copy(o, o).start()
+
+    for c in ins[:4]:
+        c.wait()
+    for j in range(QL):
+        stage[j * S : (j + 1) * S, :] = qv[:, j * HD : (j + 1) * HD].astype(F32)
+    for j in range(KV):
+        stage[(QL + j) * S : (QL + j + 1) * S, :] = nkv[:, j * HD : (j + 1) * HD].astype(F32)
+        stage[(QL + KV + j) * S : (QL + KV + j + 1) * S, :] = nvv[
+            :, j * HD : (j + 1) * HD
+        ].astype(F32)
+    xq[p] = stage[...].astype(BF)
+
+    pl.semaphore_wait(barrier, len(everyone))
+
+    def send(src, dst, ssem, rsem, to):
+        c = pltpu.make_async_remote_copy(
+            src_ref=src, dst_ref=dst, send_sem=ssem, recv_sem=rsem,
+            device_id=to, device_id_type=MESH,
+        )
+        c.start()
+        return c
+
+    sent = []
+    q_copies = [
+        send(xq.at[p], xq.at[p], q_send.at[d], q_recv.at[d], at(d, 0, 0))
+        for d in range(1, NP)
+    ]
+    sent += q_copies
+    for i, d in enumerate(everyone):
+        sent.append(send(gains.at[me], gains.at[me], g_send.at[i], g_recv.at[me], at(*d)))
+
+    slots = [slot_ref[r] for r in range(R)]
+    lengths = [len_ref[r] for r in range(R)]
+    rows_q = iota((S * QL, NP * QL * S), 0)
+    cols_q = iota((S * QL, NP * QL * S), 1)
+    req_q = (cols_q // (QL * S)) * S + cols_q % S
+    hot_q = jnp.where(
+        ((cols_q // S) % QL == rows_q % QL) & (pick(req_q, slots) == p * S + rows_q // QL),
+        1.0,
+        0.0,
+    ).astype(BF)
+    M2 = 2 * KV * S
+    rows_k = iota((2 * S * QL, NP * M2), 0)
+    cols_k = iota((2 * S * QL, NP * M2), 1)
+    req_k = (cols_k // M2) * S + cols_k % S
+    hot_k = jnp.where(
+        ((cols_k // S) % (2 * KV) == (rows_k // (S * QL)) * KV + (rows_k % QL) // G)
+        & (pick(req_k, slots) == p * S + (rows_k % (S * QL)) // QL),
+        1.0,
+        0.0,
+    ).astype(BF)
+    position = h * SPAN + iota((G, SPAN), 1)
+    live = []
+    for s in range(S):
+        length = jnp.int32(0)
+        for r in range(R):
+            length = length + jnp.where(slots[r] == p * S + s, lengths[r], 0)
+        live.append(position < length)
+
+    for c in q_copies:
+        c.wait_recv()
+    Xq = xq[:, 0 : QL * S, :].reshape(NP * QL * S, HD)
+    Xk = xq[:, QL * S :, :].reshape(NP * M2, HD)
+    Qs = mm(hot_q, Xq)
+    KVs = mm(hot_k, Xk)
+    own = jnp.exp(jnp.sum(Qs * KVs[: S * QL], axis=1, keepdims=True) * scale)
+    own = own * jnp.where(h == 0, 1.0, 0.0)
+
+    for c in ins[5:]:
+        c.wait()
+    total_parts, mixed_parts = [], []
+    for s in range(S):
+        for k in range(KV):
+            at_row = (s * KV + k) * G
+            query = Qs[at_row : at_row + G].astype(BF)
+            scores = lax.dot_general(
+                query,
+                ck[s, :, k * HD : (k + 1) * HD],
+                (((1,), (1,)), ((), ())),
+                preferred_element_type=F32,
+            )
+            weights = jnp.where(live[s], jnp.exp(scores * scale), 0.0)
+            total_parts.append(jnp.sum(weights, axis=1, keepdims=True))
+            mixed_parts.append(mm(weights.astype(BF), cv[s, :, k * HD : (k + 1) * HD]))
+    total = jnp.concatenate(total_parts, axis=0) + own
+    mixed = jnp.concatenate(mixed_parts, axis=0) + own * KVs[S * QL :]
+    B = S * HO
+    diag = iota((B, HD), 0) == iota((B, HD), 1)
+    lines = iota((16, HD), 0)
+    for t in range(NH):
+        column = []
+        for s in range(S):
+            first = s * QL + t * HO
+            send2[t, s * HO : (s + 1) * HO, :] = mixed[first : first + HO].astype(BF)
+            column.append(total[first : first + HO])
+        column = jnp.concatenate(column, axis=0)
+        line = jnp.sum(jnp.where(diag, column, 0.0), axis=0, keepdims=True)
+        high = line.astype(BF).astype(F32)
+        send2[t, B:, :] = jnp.where(
+            lines == 0, high, jnp.where(lines == 1, line - high, 0.0)
+        ).astype(BF)
+    here = p * NH + h
+    recv2[here] = send2[h]
+    a_copies = []
+    for i, (dp, dh, da) in enumerate([d for d in everyone if d[2] == 0]):
+        to = at(dp, dh, 0)
+        a_copies.append(
+            send(send2.at[to["head"]], recv2.at[here], a_send.at[i], a_recv.at[i], to)
+        )
+    sent += a_copies
+
+    RH = iota((HO * R, NP * B), 0)
+    CH = iota((HO * R, NP * B), 1)
+    order = jnp.where(
+        (RH // R == CH % HO) & (pick(RH % R, slots) == CH // HO), 1.0, 0.0
+    ).astype(BF)
+    for c in a_copies:
+        c.wait_recv()
+    attended = []
+    for q in range(NP):
+        got = recv2[q * NH].astype(F32)
+        for t in range(1, NH):
+            got = got + recv2[q * NH + t].astype(F32)
+        line = got[B : B + 1] + got[B + 1 : B + 2]
+        column = jnp.sum(jnp.where(diag, line, 0.0), axis=1, keepdims=True)
+        attended.append((got[:B] / column).astype(BF))
+    by_head = mm(order, jnp.concatenate(attended, axis=0))
+    by_request = jnp.concatenate(
+        [by_head[j * R : (j + 1) * R] for j in range(HO)], axis=1
+    ).astype(BF)
+
+    for c in wo_copies:
+        c.wait()
+    mine = h * NA + a
+    for n in range(QUAD):
+        term = jnp.zeros((R, W), F32)
+        for slot, lane, row in wo_places:
+            term = term + mm(
+                by_request[:, row : row + ROWS], ring[slot, :, lane + n * W : lane + (n + 1) * W]
+            )
+        send3[n] = term
+    recv3[mine] = send3[mine]
+    t_copies = []
+    for i, (dp, dh, da) in enumerate([d for d in everyone if d[0] == 0]):
+        to = at(0, dh, da)
+        t_copies.append(
+            send(
+                send3.at[to["head"] * NA + to["aux"]],
+                recv3.at[mine],
+                t_send.at[i],
+                t_recv.at[i],
+                to,
+            )
+        )
+    sent += t_copies
+    for o in range(NBUF - held_slots, NBUF):
+        lm_copy(o, o).start()
+    ins[4].wait()
+    for c in t_copies:
+        c.wait_recv()
+    stream = hid[...].astype(F32)
+    projected = recv3[0]
+    for n in range(1, QUAD):
+        projected = projected + recv3[n]
+    stream = stream + projected
+    xs[me] = jnp.concatenate([stream[:, : W // 2], stream[:, W // 2 :]], axis=0).astype(BF)
+    for i, d in enumerate(everyone):
+        sent.append(send(xs.at[me], xs.at[me], s_send.at[i], s_recv.at[me], at(*d)))
+
+    acc[...] = jnp.zeros_like(acc)
+
+    def step(o, squares):
+        b = block_of(o)
+        slot = lax.rem(o, NBUF)
+
+        @pl.when(b != me)
+        def _():
+            pltpu.make_async_remote_copy(
+                src_ref=gains.at[b], dst_ref=gains.at[b], send_sem=g_send.at[0],
+                recv_sem=g_recv.at[b], device_id=at(1, 0, 0), device_id_type=MESH,
+            ).wait_recv()
+            pltpu.make_async_remote_copy(
+                src_ref=xs.at[b], dst_ref=xs.at[b], send_sem=s_send.at[0],
+                recv_sem=s_recv.at[b], device_id=at(1, 0, 0), device_id_type=MESH,
+            ).wait_recv()
+
+        halves = xs[b].astype(F32)
+        block = jnp.concatenate([halves[:R], halves[R:]], axis=1)
+        left = (block * gains[b]).astype(BF)
+        lm_copy(o, slot).wait()
+        acc[...] += mm(left, ring[slot])
+
+        @pl.when(o + NBUF < NCH)
+        def _():
+            lm_copy(o + NBUF, slot).start()
+
+        return squares + jnp.sum(block * block, axis=1, keepdims=True)
+
+    squares = lax.fori_loop(0, NCH, step, jnp.zeros((R, 1), F32))
+    logits = acc[...] * lax.rsqrt(squares * (1.0 / (NCH * ROWS)) + 1e-05)
+    acc[...] = logits
+    out = pltpu.make_async_copy(acc, logits_hbm, out_sem)
+    out.start()
+    expd = jnp.exp(logits)
+    sums = jnp.sum(expd, axis=1, keepdims=True)
+    moments = jnp.sum(expd * logits, axis=1, keepdims=True)
+    lane = iota((R, HD), 1)
+    xe[me] = jnp.where(lane == 0, sums, jnp.where(lane == 1, moments, 0.0))
+    e_copies = [
+        send(xe.at[me], xe.at[me], e_send.at[i], e_recv.at[i], at(*d))
+        for i, d in enumerate(everyone)
+    ]
+    sent += e_copies
+    for c in e_copies:
+        c.wait_recv()
+    both = jnp.sum(xe[...], axis=0)
+    vocab_total, moment = both[:, 0:1], both[:, 1:2]
+    entropy = jnp.log(vocab_total) - moment / vocab_total
+    spread = jnp.sum(jnp.where(iota((R, HD), 0) == lane, entropy, 0.0), axis=0, keepdims=True)
+    ent_ref[...] = spread[:, :R]
+    out.wait()
+    for c in sent:
+        c.wait_send()
+
+
+def one_kernel(
+    cfg,
+    hidden, gain, queries, new_key, new_value, cache_key, cache_value, lengths, slot_of,
+    out_proj, lm_head,
+):
+    NP, NH, NA = cfg["NP"], cfg["NH"], cfg["NA"]
+    R, S, KV, G, SPAN = cfg["R"], cfg["S"], cfg["KV"], cfg["G"], cfg["SPAN"]
+    W, NCH, NBUF = cfg["W"], cfg["NCH"], cfg["NBUF"]
+    QL = KV * G
+    N = NP * NH * NA
+    QUAD = NH * NA
+    VL = lm_head.shape[1]
+    rows = (QL + 2 * KV) * S
+    message = S * (QL // NH) + 16
+    DMA = pltpu.SemaphoreType.DMA
+    smem = pl.BlockSpec(memory_space=pltpu.SMEM)
+    anywhere = pl.BlockSpec(memory_space=pl.ANY)
+    weights = lm_head.size + out_proj.size + 2 * cache_key.size
+    logits, entropy = pl.pallas_call(
+        functools.partial(kernel, cfg),
+        out_shape=(
+            jax.ShapeDtypeStruct((R, VL), F32),
+            jax.ShapeDtypeStruct((1, R), F32),
+        ),
+        in_specs=[smem, smem] + [anywhere] * 9,
+        out_specs=(anywhere, pl.BlockSpec(memory_space=pltpu.VMEM)),
+        scratch_shapes=[
+            pltpu.VMEM((NBUF, W, VL), BF),
+            pltpu.VMEM(cache_key.shape, BF),
+            pltpu.VMEM(cache_value.shape, BF),
+            pltpu.VMEM(queries.shape, BF),
+            pltpu.VMEM(new_key.shape, BF),
+            pltpu.VMEM(new_value.shape, BF),
+            pltpu.VMEM(hidden.shape, BF),
+            pltpu.VMEM((N, 1, W), F32),
+            pltpu.VMEM((rows, HD), F32),
+            pltpu.VMEM((NP, rows, HD), BF),
+            pltpu.VMEM((NH, message, HD), BF),
+            pltpu.VMEM((NP * NH, message, HD), BF),
+            pltpu.VMEM((QUAD, R, W), F32),
+            pltpu.VMEM((QUAD, R, W), F32),
+            pltpu.VMEM((N, 2 * R, W // 2), BF),
+            pltpu.VMEM((R, VL), F32),
+            pltpu.VMEM((N, R, HD), F32),
+            DMA((NBUF,)),
+            DMA((out_proj.shape[1] // W,)),
+            DMA((7,)),
+            DMA,
+            DMA((NP,)),
+            DMA((NP,)),
+            DMA((N,)),
+            DMA((N,)),
+            DMA((NP * NH,)),
+            DMA((NP * NH,)),
+            DMA((QUAD,)),
+            DMA((QUAD,)),
+            DMA((N,)),
+            DMA((N,)),
+            DMA((N,)),
+            DMA((N,)),
+        ],
+        compiler_params=pltpu.CompilerParams(
+            collective_id=0, has_side_effects=True, vmem_limit_bytes=63 * MIB
+        ),
+        cost_estimate=pl.CostEstimate(
+            flops=2 * R * weights, bytes_accessed=2 * weights, transcendentals=R * VL
+        ),
+    )(
+        slot_of, lengths, hidden, gain.reshape(1, W), queries, new_key, new_value,
+        cache_key, cache_value, out_proj, lm_head,
+    )
+    return logits, entropy.reshape(R)
+
+
+def arrangement(mesh, args):
+    NP, NH, NA = mesh.shape["pool"], mesh.shape["head"], mesh.shape["aux"]
+    hidden, queries, cache_key, out_proj, lm_head = (
+        args[0], args[2], args[5], args[9], args[10],
+    )
+    R, W = hidden.shape
+    S, SPAN = cache_key.shape[:2]
+    KV = cache_key.shape[2] // HD
+    QL = queries.shape[1] // HD
+    VL = lm_head.shape[1]
+    HO = out_proj.shape[1] // HD
+    fits = (
+        R == 8
+        and W % 256 == 0
+        and VL % out_proj.shape[2] == 0
+        and out_proj.shape[1] % W == 0
+        and (out_proj.shape[1] // W) % (VL // out_proj.shape[2]) == 0
+        and HO % 16 == 0
+        and S * HO <= HD
+        and QL // KV == 8
+        and (KV * S) % 8 == 0
+        and SPAN % 128 == 0
+        and W * VL * 2 * RING <= 60 * MIB
+    )
+    if not fits:
+        return None
+    return dict(
+        NP=NP, NH=NH, NA=NA, R=R, S=S, KV=KV, G=QL // KV, SPAN=SPAN, W=W,
+        NCH=lm_head.shape[0] // W, NBUF=min(RING, lm_head.shape[0] // W),
+    )
 
 
 def select_rows(onehot, rows):
@@ -128,6 +612,13 @@
         P(None, ("pool", "head", "aux")),
     )
     out_specs = (P("grp", ("pool", "head", "aux")), P("grp"))
+
+    def on_device(*args):
+        cfg = arrangement(mesh, args)
+        if cfg is None:
+            return per_device(*args)
+        return one_kernel(cfg, *args)
+
     return jax.shard_map(
-        per_device, mesh=mesh, in_specs=in_specs, out_specs=out_specs, check_vma=False
-    )
+        on_device, mesh=mesh, in_specs=in_specs, out_specs=out_specs, check_vma=False
+    )

time: 174 us -> 56.5 us (0.32)
  blocking collectives: 138 us -> 0 us
  Pallas kernels: 0 us -> 53 us
  matrix products: 32.3 us -> 0 us
  other arithmetic: 2.71 us -> 0 us
  local copies, waits for them, and re-layouts: 0.26 us -> 2.74 us
    all_gather x8 -> x0, blocking collectives: 89.4 us -> none  [the longest x1 13.5 us: per_device(): lax.all_gather(stream, 'pool', axis=1, tiled=True)]
    pallas_call x0 -> x1, Pallas kernels: none -> 53 us  [one_kernel(): pl.pallas_call(functools.partial(kernel, cfg), out_shape=(jax.ShapeDtypeS...]
    psum x3 -> x0, blocking collectives: 48.2 us -> none  [the longest x1 29.5 us: per_device(): lax.psum((jnp.sum(expd, axis=1), jnp.sum(expd * logits, axis=1)), ('pool'...]
    dot_general x7 -> x0, matrix products: 32.3 us -> none  [the longest x1 23.5 us: per_device(): logits = jnp.dot(normed, lm_head, preferred_element_type=jnp.float32)]
    unnamed x10 -> x2, local copies, waits for them, and re-layouts: 0.14 us -> 2.74 us
where the time goes in v1:
time: 56.5 us; the launch traced here: 56.3 us
  Pallas kernels  53 us (94%)
  local copies, waits for them, and re-layouts  2.74 us (5%)
  between operations  0.64 us (1%)
    pallas_call x1, Pallas kernels, one_kernel(): pl.pallas_call(functools.partial(kernel, cfg), out_shape=(jax.ShapeDtypeS...  53 us
    unnamed x2, local copies, waits for them, and re-layouts  2.74 us

profile of v1, /device:TPU:0, one launch (start us, length us, event | category | flops | bytes accessed | tf_op | source)
XLA Modules:
  0.0 56.3 jit_solution(2159432602678236606)
XLA Ops:
  0.6 53.0 %shard_map.122 = (f32[8,4096]{1,0:T(8,128)}, f32[1,8]{1,0:T(1,128)}) custom-call(s32[8]{0:T(128)} %slot_ref.1, s32[8]{0:T(128)} %len_ref.1, bf16[8,512]{1,0:T(8,128)(2,1)} %hidden_hbm.1, f32[1,512]{1,0:T(1,128)} %bitcast.2, bf16[2,4096]{1,0:T(2,128)(2,1)} %q_hbm.1, bf16[2,512]{1,0:T(2,128)(2,1)} %nk_hbm.1, bf16[2,512]{1,0:T(2,128)(2,1)} %nv_hbm.1, ...), custom_call_target="tpu_custom_call" | custom-call | flops 612368384 | bytes 76546048 | tf_op jit(solution)/shard_map/pallas_call | solution.py:407
  53.6 1.6 %copy.15 = f32[8,4096]{1,0:T(8,128)} copy(f32[8,4096]{1,0:T(8,128)} %get-tuple-element.8) | data formatting | bytes 262144
  55.2 1.2 %copy.16 = f32[8]{0:T(128)} copy(f32[8]{0:T(128)} %bitcast.3) | data formatting | bytes 64

commit v2 on v1

--- a/solution.py
+++ b/solution.py
@@ -159,8 +159,13 @@
             lm_hbm.at[pl.ds(row, ROWS), :], ring.at[slot], ring_sem.at[slot]
         )
 
-    for o in range(NBUF - held_slots):
-        lm_copy(o, o).start()
+    free = NBUF - held_slots
+
+    def start_chunks(first, last):
+        for o in range(min(first, free), min(last, free)):
+            lm_copy(o, o).start()
+
+    start_chunks(0, 2)
 
     for c in ins[:4]:
         c.wait()
@@ -222,6 +227,7 @@
 
     for c in q_copies:
         c.wait_recv()
+    start_chunks(2, 6)
     Xq = xq[:, 0 : QL * S, :].reshape(NP * QL * S, HD)
     Xk = xq[:, QL * S :, :].reshape(NP * M2, HD)
     Qs = mm(hot_q, Xq)
@@ -279,6 +285,7 @@
     ).astype(BF)
     for c in a_copies:
         c.wait_recv()
+    start_chunks(6, 10)
     attended = []
     for q in range(NP):
         got = recv2[q * NH].astype(F32)
@@ -316,8 +323,6 @@
             )
         )
     sent += t_copies
-    for o in range(NBUF - held_slots, NBUF):
-        lm_copy(o, o).start()
     ins[4].wait()
     for c in t_copies:
         c.wait_recv()
@@ -329,6 +334,9 @@
     xs[me] = jnp.concatenate([stream[:, : W // 2], stream[:, W // 2 :]], axis=0).astype(BF)
     for i, d in enumerate(everyone):
         sent.append(send(xs.at[me], xs.at[me], s_send.at[i], s_recv.at[me], at(*d)))
+    start_chunks(10, free)
+    for o in range(free, NBUF):
+        lm_copy(o, o).start()
 
     acc[...] = jnp.zeros_like(acc)
 
@@ -384,6 +392,13 @@
     out.wait()
     for c in sent:
         c.wait_send()
+
+
+def closing(logits_in, ent_in, logits_out, ent_out, sem):
+    copy = pltpu.make_async_copy(logits_in, logits_out, sem)
+    copy.start()
+    ent_out[...] = ent_in[...]
+    copy.wait()
 
 
 def one_kernel(
@@ -457,6 +472,16 @@
         slot_of, lengths, hidden, gain.reshape(1, W), queries, new_key, new_value,
         cache_key, cache_value, out_proj, lm_head,
     )
+    logits, entropy = pl.pallas_call(
+        closing,
+        out_shape=(
+            jax.ShapeDtypeStruct((R, VL), F32),
+            jax.ShapeDtypeStruct((1, R), F32),
+        ),
+        in_specs=[anywhere, pl.BlockSpec(memory_space=pltpu.VMEM)],
+        out_specs=(anywhere, pl.BlockSpec(memory_space=pltpu.VMEM)),
+        scratch_shapes=[DMA],
+    )(logits, entropy)
     return logits, entropy.reshape(R)
 
 

time: 56.5 us -> 48.2 us (0.85)
  Pallas kernels: 53 us -> 47.3 us
  local copies, waits for them, and re-layouts: 2.74 us -> 0 us
    pallas_call x1, Pallas kernels: 53 us -> 41.1 us  [one_kernel(): pl.pallas_call(functools.partial(kernel, cfg), out_shape=(jax.ShapeDtypeS...]
    pallas_call x0 -> x1, Pallas kernels: none -> 6.24 us  [one_kernel(): pl.pallas_call(closing, out_shape=(jax.ShapeDtypeStruct((R, VL), F32), ja...]
    unnamed x2 -> x0, local copies, waits for them, and re-layouts: 2.74 us -> none
where the time goes in v2:
time: 48.2 us; the launch traced here: 48 us
  Pallas kernels  47.3 us (98%)
  between operations  0.64 us (1%)
    pallas_call x1, Pallas kernels, one_kernel(): pl.pallas_call(functools.partial(kernel, cfg), out_shape=(jax.ShapeDtypeS...  41.1 us
    pallas_call x1, Pallas kernels, one_kernel(): pl.pallas_call(closing, out_shape=(jax.ShapeDtypeStruct((R, VL), F32), ja...  6.24 us

profile of v2, /device:TPU:0, one launch (start us, length us, event | category | flops | bytes accessed | tf_op | source)
XLA Modules:
  0.0 48.0 jit_solution(6306960430118597308)
XLA Ops:
  0.6 41.1 %shard_map.122 = (f32[8,4096]{1,0:T(8,128)}, f32[1,8]{1,0:T(1,128)}) custom-call(s32[8]{0:T(128)} %slot_ref.1, s32[8]{0:T(128)} %len_ref.1, bf16[8,512]{1,0:T(8,128)(2,1)} %hidden_hbm.1, f32[1,512]{1,0:T(1,128)} %bitcast.2, bf16[2,4096]{1,0:T(2,128)(2,1)} %q_hbm.1, bf16[2,512]{1,0:T(2,128)(2,1)} %nk_hbm.1, bf16[2,512]{1,0:T(2,128)(2,1)} %nv_hbm.1, ...), custom_call_target="tpu_custom_call" | custom-call | flops 612368384 | bytes 76546048 | tf_op jit(solution)/shard_map/pallas_call | solution.py:422
  41.7 6.2 %shard_map.123 = (f32[8,4096]{1,0:T(8,128)}, f32[1,8]{1,0:T(1,128)}) custom-call(f32[8,4096]{1,0:T(8,128)} %get-tuple-element.6.logits_in, f32[1,8]{1,0:T(1,128)} %get-tuple-element.7.ent_in), custom_call_target="tpu_custom_call" | custom-call | tf_op jit(solution)/shard_map/pallas_call | solution.py:475

commit v3 on v2

--- a/solution.py
+++ b/solution.py
@@ -61,6 +61,7 @@
     send3,
     recv3,
     xs,
+    lefts,
     acc,
     xe,
     ring_sem,
@@ -163,7 +164,7 @@
 
     def start_chunks(first, last):
         for o in range(min(first, free), min(last, free)):
-            lm_copy(o, o).start()
+            lm_copy(o, o).start(priority=1)
 
     start_chunks(0, 2)
 
@@ -196,6 +197,7 @@
     sent += q_copies
     for i, d in enumerate(everyone):
         sent.append(send(gains.at[me], gains.at[me], g_send.at[i], g_recv.at[me], at(*d)))
+    start_chunks(2, 4)
 
     slots = [slot_ref[r] for r in range(R)]
     lengths = [len_ref[r] for r in range(R)]
@@ -227,7 +229,6 @@
 
     for c in q_copies:
         c.wait_recv()
-    start_chunks(2, 6)
     Xq = xq[:, 0 : QL * S, :].reshape(NP * QL * S, HD)
     Xk = xq[:, QL * S :, :].reshape(NP * M2, HD)
     Qs = mm(hot_q, Xq)
@@ -277,6 +278,7 @@
             send(send2.at[to["head"]], recv2.at[here], a_send.at[i], a_recv.at[i], to)
         )
     sent += a_copies
+    start_chunks(4, 6)
 
     RH = iota((HO * R, NP * B), 0)
     CH = iota((HO * R, NP * B), 1)
@@ -285,7 +287,6 @@
     ).astype(BF)
     for c in a_copies:
         c.wait_recv()
-    start_chunks(6, 10)
     attended = []
     for q in range(NP):
         got = recv2[q * NH].astype(F32)
@@ -302,26 +303,23 @@
     for c in wo_copies:
         c.wait()
     mine = h * NA + a
-    for n in range(QUAD):
+    t_copies = []
+    for i in range(1, QUAD + 1):
+        n = lax.rem(mine + i, QUAD)
         term = jnp.zeros((R, W), F32)
         for slot, lane, row in wo_places:
-            term = term + mm(
-                by_request[:, row : row + ROWS], ring[slot, :, lane + n * W : lane + (n + 1) * W]
+            part = pl.ds(pl.multiple_of(lane + n * W, W), W)
+            term = term + mm(by_request[:, row : row + ROWS], ring[slot, :, part])
+        if i == QUAD:
+            recv3[mine] = term
+        else:
+            send3[n] = term
+            to = {"pool": p, "head": n // NA, "aux": lax.rem(n, NA)}
+            t_copies.append(
+                send(send3.at[n], recv3.at[mine], t_send.at[i], t_recv.at[i], to)
             )
-        send3[n] = term
-    recv3[mine] = send3[mine]
-    t_copies = []
-    for i, (dp, dh, da) in enumerate([d for d in everyone if d[0] == 0]):
-        to = at(0, dh, da)
-        t_copies.append(
-            send(
-                send3.at[to["head"] * NA + to["aux"]],
-                recv3.at[mine],
-                t_send.at[i],
-                t_recv.at[i],
-                to,
-            )
-        )
+            if i == QUAD - 1:
+                start_chunks(6, 8)
     sent += t_copies
     ins[4].wait()
     for c in t_copies:
@@ -334,40 +332,50 @@
     xs[me] = jnp.concatenate([stream[:, : W // 2], stream[:, W // 2 :]], axis=0).astype(BF)
     for i, d in enumerate(everyone):
         sent.append(send(xs.at[me], xs.at[me], s_send.at[i], s_recv.at[me], at(*d)))
-    start_chunks(10, free)
+    start_chunks(8, free)
     for o in range(free, NBUF):
-        lm_copy(o, o).start()
+        lm_copy(o, o).start(priority=1)
 
     acc[...] = jnp.zeros_like(acc)
 
-    def step(o, squares):
-        b = block_of(o)
-        slot = lax.rem(o, NBUF)
-
-        @pl.when(b != me)
-        def _():
-            pltpu.make_async_remote_copy(
-                src_ref=gains.at[b], dst_ref=gains.at[b], send_sem=g_send.at[0],
-                recv_sem=g_recv.at[b], device_id=at(1, 0, 0), device_id_type=MESH,
-            ).wait_recv()
-            pltpu.make_async_remote_copy(
-                src_ref=xs.at[b], dst_ref=xs.at[b], send_sem=s_send.at[0],
-                recv_sem=s_recv.at[b], device_id=at(1, 0, 0), device_id_type=MESH,
-            ).wait_recv()
-
-        halves = xs[b].astype(F32)
-        block = jnp.concatenate([halves[:R], halves[R:]], axis=1)
-        left = (block * gains[b]).astype(BF)
-        lm_copy(o, slot).wait()
-        acc[...] += mm(left, ring[slot])
-
-        @pl.when(o + NBUF < NCH)
-        def _():
-            lm_copy(o + NBUF, slot).start()
-
-        return squares + jnp.sum(block * block, axis=1, keepdims=True)
-
-    squares = lax.fori_loop(0, NCH, step, jnp.zeros((R, 1), F32))
+    def arrived(block, sems):
+        return pltpu.make_async_remote_copy(
+            src_ref=block, dst_ref=block, send_sem=s_send.at[0], recv_sem=sems,
+            device_id=at(1, 0, 0), device_id_type=MESH,
+        )
+
+    def group(g, squares):
+        for i in range(QUAD):
+            b = block_of(g * QUAD + i)
+
+            @pl.when(b != me)
+            def _():
+                arrived(gains.at[b], g_recv.at[b]).wait_recv()
+                arrived(xs.at[b], s_recv.at[b]).wait_recv()
+
+        for i in range(QUAD):
+            b = block_of(g * QUAD + i)
+            halves = xs[b].astype(F32)
+            block = jnp.concatenate([halves[:R], halves[R:]], axis=1)
+            lefts[i] = (block * gains[b]).astype(BF)
+            squares = squares + jnp.sum(block * block, axis=1, keepdims=True)
+
+        def step(i, none):
+            o = g * QUAD + i
+            slot = lax.rem(o, NBUF)
+            lm_copy(o, slot).wait()
+            acc[...] += mm(lefts[i], ring[slot])
+
+            @pl.when(o + NBUF < NCH)
+            def _():
+                lm_copy(o + NBUF, slot).start(priority=1)
+
+            return none
+
+        lax.fori_loop(0, QUAD, step, 0)
+        return squares
+
+    squares = lax.fori_loop(0, NCH // QUAD, group, jnp.zeros((R, 1), F32))
     logits = acc[...] * lax.rsqrt(squares * (1.0 / (NCH * ROWS)) + 1e-05)
     acc[...] = logits
     out = pltpu.make_async_copy(acc, logits_hbm, out_sem)
@@ -443,6 +451,7 @@
             pltpu.VMEM((QUAD, R, W), F32),
             pltpu.VMEM((QUAD, R, W), F32),
             pltpu.VMEM((N, 2 * R, W // 2), BF),
+            pltpu.VMEM((QUAD, R, W), BF),
             pltpu.VMEM((R, VL), F32),
             pltpu.VMEM((N, R, HD), F32),
             DMA((NBUF,)),

time: 48.2 us -> 48.1 us (level)
  no operation moved by 1% of the time
where the time goes in v3:
time: 48.1 us; the launch traced here: 47.9 us
  Pallas kernels  47.2 us (98%)
  between operations  0.64 us (1%)
    pallas_call x1, Pallas kernels, one_kernel(): pl.pallas_call(functools.partial(kernel, cfg), out_shape=(jax.ShapeDtypeS...  41 us
    pallas_call x1, Pallas kernels, one_kernel(): pl.pallas_call(closing, out_shape=(jax.ShapeDtypeStruct((R, VL), F32), ja...  6.24 us

profile of v3, /device:TPU:0, one launch (start us, length us, event | category | flops | bytes accessed | tf_op | source)
XLA Modules:
  0.0 47.9 jit_solution(18133734187250026795)
XLA Ops:
  0.6 41.0 %shard_map.122 = (f32[8,4096]{1,0:T(8,128)}, f32[1,8]{1,0:T(1,128)}) custom-call(s32[8]{0:T(128)} %slot_ref.1, s32[8]{0:T(128)} %len_ref.1, bf16[8,512]{1,0:T(8,128)(2,1)} %hidden_hbm.1, f32[1,512]{1,0:T(1,128)} %bitcast.2, bf16[2,4096]{1,0:T(2,128)(2,1)} %q_hbm.1, bf16[2,512]{1,0:T(2,128)(2,1)} %nk_hbm.1, bf16[2,512]{1,0:T(2,128)(2,1)} %nv_hbm.1, ...), custom_call_target="tpu_custom_call" | custom-call | flops 612368384 | bytes 76546048 | tf_op jit(solution)/shard_map/pallas_call | solution.py:430
  41.6 6.2 %shard_map.123 = (f32[8,4096]{1,0:T(8,128)}, f32[1,8]{1,0:T(1,128)}) custom-call(f32[8,4096]{1,0:T(8,128)} %get-tuple-element.6.logits_in, f32[1,8]{1,0:T(1,128)} %get-tuple-element.7.ent_in), custom_call_target="tpu_custom_call" | custom-call | tf_op jit(solution)/shard_map/pallas_call | solution.py:484

commit v4 on v3

--- a/solution.py
+++ b/solution.py
@@ -48,6 +48,7 @@
     ent_ref,
     ring,
     ck,
+    kt,
     cv,
     qv,
     nkv,
@@ -58,10 +59,9 @@
     xq,
     send2,
     recv2,
-    send3,
+    hidden_quad,
     recv3,
     xs,
-    lefts,
     acc,
     xe,
     ring_sem,
@@ -76,6 +76,8 @@
     a_recv,
     t_send,
     t_recv,
+    h_send,
+    h_recv,
     s_send,
     s_recv,
     e_send,
@@ -168,7 +170,7 @@
 
     start_chunks(0, 2)
 
-    for c in ins[:4]:
+    for c in ins[:5]:
         c.wait()
     for j in range(QL):
         stage[j * S : (j + 1) * S, :] = qv[:, j * HD : (j + 1) * HD].astype(F32)
@@ -178,6 +180,8 @@
             :, j * HD : (j + 1) * HD
         ].astype(F32)
     xq[p] = stage[...].astype(BF)
+    mine = h * NA + a
+    hidden_quad[mine] = hid[...].astype(F32)
 
     pl.semaphore_wait(barrier, len(everyone))
 
@@ -197,6 +201,12 @@
     sent += q_copies
     for i, d in enumerate(everyone):
         sent.append(send(gains.at[me], gains.at[me], g_send.at[i], g_recv.at[me], at(*d)))
+    quad = [d for d in everyone if d[0] == 0]
+    h_copies = [
+        send(hidden_quad.at[mine], hidden_quad.at[mine], h_send.at[i], h_recv.at[i], at(*d))
+        for i, d in enumerate(quad)
+    ]
+    sent += h_copies
     start_chunks(2, 4)
 
     slots = [slot_ref[r] for r in range(R)]
@@ -227,6 +237,10 @@
             length = length + jnp.where(slots[r] == p * S + s, lengths[r], 0)
         live.append(position < length)
 
+    ins[5].wait()
+    for s in range(S):
+        kt[s] = ck[s].T
+
     for c in q_copies:
         c.wait_recv()
     Xq = xq[:, 0 : QL * S, :].reshape(NP * QL * S, HD)
@@ -236,19 +250,13 @@
     own = jnp.exp(jnp.sum(Qs * KVs[: S * QL], axis=1, keepdims=True) * scale)
     own = own * jnp.where(h == 0, 1.0, 0.0)
 
-    for c in ins[5:]:
-        c.wait()
+    ins[6].wait()
     total_parts, mixed_parts = [], []
     for s in range(S):
         for k in range(KV):
             at_row = (s * KV + k) * G
             query = Qs[at_row : at_row + G].astype(BF)
-            scores = lax.dot_general(
-                query,
-                ck[s, :, k * HD : (k + 1) * HD],
-                (((1,), (1,)), ((), ())),
-                preferred_element_type=F32,
-            )
+            scores = mm(query, kt[s, k * HD : (k + 1) * HD, :])
             weights = jnp.where(live[s], jnp.exp(scores * scale), 0.0)
             total_parts.append(jnp.sum(weights, axis=1, keepdims=True))
             mixed_parts.append(mm(weights.astype(BF), cv[s, :, k * HD : (k + 1) * HD]))
@@ -302,36 +310,40 @@
 
     for c in wo_copies:
         c.wait()
-    mine = h * NA + a
-    t_copies = []
-    for i in range(1, QUAD + 1):
-        n = lax.rem(mine + i, QUAD)
+    terms = []
+    for n in range(QUAD):
         term = jnp.zeros((R, W), F32)
         for slot, lane, row in wo_places:
-            part = pl.ds(pl.multiple_of(lane + n * W, W), W)
-            term = term + mm(by_request[:, row : row + ROWS], ring[slot, :, part])
-        if i == QUAD:
-            recv3[mine] = term
-        else:
-            send3[n] = term
-            to = {"pool": p, "head": n // NA, "aux": lax.rem(n, NA)}
-            t_copies.append(
-                send(send3.at[n], recv3.at[mine], t_send.at[i], t_recv.at[i], to)
-            )
-            if i == QUAD - 1:
-                start_chunks(6, 8)
+            first = lane + n * W
+            term = term + mm(by_request[:, row : row + ROWS], ring[slot, :, first : first + W])
+        terms.append(term)
+
+    def two_rows(blocks):
+        half = len(blocks) // 2
+        return jnp.concatenate(
+            [jnp.concatenate(blocks[:half], axis=1), jnp.concatenate(blocks[half:], axis=1)],
+            axis=0,
+        )
+
+    recv3[mine] = two_rows(terms).astype(BF)
+    t_copies = [
+        send(recv3.at[mine], recv3.at[mine], t_send.at[i], t_recv.at[i], at(*d))
+        for i, d in enumerate(quad)
+    ]
     sent += t_copies
-    ins[4].wait()
+    start_chunks(6, 8)
+    for c in h_copies:
+        c.wait_recv()
+    stream = two_rows([hidden_quad[n] for n in range(QUAD)])
     for c in t_copies:
         c.wait_recv()
-    stream = hid[...].astype(F32)
-    projected = recv3[0]
+    projected = recv3[0].astype(F32)
     for n in range(1, QUAD):
-        projected = projected + recv3[n]
-    stream = stream + projected
-    xs[me] = jnp.concatenate([stream[:, : W // 2], stream[:, W // 2 :]], axis=0).astype(BF)
-    for i, d in enumerate(everyone):
-        sent.append(send(xs.at[me], xs.at[me], s_send.at[i], s_recv.at[me], at(*d)))
+        projected = projected + recv3[n].astype(F32)
+    xs[p] = (stream + projected).astype(BF)
+    sent += [
+        send(xs.at[p], xs.at[p], s_send.at[d], s_recv.at[p], at(d, 0, 0)) for d in range(1, NP)
+    ]
     start_chunks(8, free)
     for o in range(free, NBUF):
         lm_copy(o, o).start(priority=1)
@@ -345,34 +357,43 @@
         )
 
     def group(g, squares):
+        q = lax.rem(p + g, NP)
+
+        @pl.when(g > 0)
+        def _():
+            arrived(xs.at[q], s_recv.at[q]).wait_recv()
+
         for i in range(QUAD):
-            b = block_of(g * QUAD + i)
+            b = q * QUAD + i
 
             @pl.when(b != me)
             def _():
                 arrived(gains.at[b], g_recv.at[b]).wait_recv()
-                arrived(xs.at[b], s_recv.at[b]).wait_recv()
-
+
+        both = xs[q].astype(F32)
+        lefts = []
         for i in range(QUAD):
-            b = block_of(g * QUAD + i)
-            halves = xs[b].astype(F32)
-            block = jnp.concatenate([halves[:R], halves[R:]], axis=1)
-            lefts[i] = (block * gains[b]).astype(BF)
+            top = (i // (QUAD // 2)) * R
+            lane = (i % (QUAD // 2)) * W
+            block = both[top : top + R, lane : lane + W]
+            lefts.append((block * gains[q * QUAD + i]).astype(BF))
             squares = squares + jnp.sum(block * block, axis=1, keepdims=True)
-
-        def step(i, none):
+        held = [lax.rem(g * QUAD + i, NBUF) for i in range(QUAD)]
+        for i in range(QUAD):
+            lm_copy(g * QUAD + i, held[i]).wait()
+        part = VL // 4
+        for first in range(0, VL, part):
+            add = mm(lefts[0], ring[held[0], :, first : first + part])
+            for i in range(1, QUAD):
+                add = add + mm(lefts[i], ring[held[i], :, first : first + part])
+            acc[:, first : first + part] += add
+        for i in range(QUAD):
             o = g * QUAD + i
-            slot = lax.rem(o, NBUF)
-            lm_copy(o, slot).wait()
-            acc[...] += mm(lefts[i], ring[slot])
 
             @pl.when(o + NBUF < NCH)
             def _():
-                lm_copy(o + NBUF, slot).start(priority=1)
-
-            return none
-
-        lax.fori_loop(0, QUAD, step, 0)
+                lm_copy(o + NBUF, held[i]).start(priority=1)
+
         return squares
 
     squares = lax.fori_loop(0, NCH // QUAD, group, jnp.zeros((R, 1), F32))
@@ -402,11 +423,9 @@
         c.wait_send()
 
 
-def closing(logits_in, ent_in, logits_out, ent_out, sem):
-    copy = pltpu.make_async_copy(logits_in, logits_out, sem)
-    copy.start()
+def closing(logits_in, ent_in, logits_out, ent_out):
+    logits_out[...] = logits_in[...]
     ent_out[...] = ent_in[...]
-    copy.wait()
 
 
 def one_kernel(
@@ -438,6 +457,7 @@
         scratch_shapes=[
             pltpu.VMEM((NBUF, W, VL), BF),
             pltpu.VMEM(cache_key.shape, BF),
+            pltpu.VMEM((S, cache_key.shape[2], SPAN), BF),
             pltpu.VMEM(cache_value.shape, BF),
             pltpu.VMEM(queries.shape, BF),
             pltpu.VMEM(new_key.shape, BF),
@@ -449,9 +469,8 @@
             pltpu.VMEM((NH, message, HD), BF),
             pltpu.VMEM((NP * NH, message, HD), BF),
             pltpu.VMEM((QUAD, R, W), F32),
-            pltpu.VMEM((QUAD, R, W), F32),
-            pltpu.VMEM((N, 2 * R, W // 2), BF),
-            pltpu.VMEM((QUAD, R, W), BF),
+            pltpu.VMEM((QUAD, 2 * R, QUAD * W // 2), BF),
+            pltpu.VMEM((NP, 2 * R, QUAD * W // 2), BF),
             pltpu.VMEM((R, VL), F32),
             pltpu.VMEM((N, R, HD), F32),
             DMA((NBUF,)),
@@ -466,8 +485,10 @@
             DMA((NP * NH,)),
             DMA((QUAD,)),
             DMA((QUAD,)),
-            DMA((N,)),
-            DMA((N,)),
+            DMA((QUAD,)),
+            DMA((QUAD,)),
+            DMA((NP,)),
+            DMA((NP,)),
             DMA((N,)),
             DMA((N,)),
         ],
@@ -487,9 +508,6 @@
             jax.ShapeDtypeStruct((R, VL), F32),
             jax.ShapeDtypeStruct((1, R), F32),
         ),
-        in_specs=[anywhere, pl.BlockSpec(memory_space=pltpu.VMEM)],
-        out_specs=(anywhere, pl.BlockSpec(memory_space=pltpu.VMEM)),
-        scratch_shapes=[DMA],
     )(logits, entropy)
     return logits, entropy.reshape(R)
 
@@ -516,6 +534,9 @@
         and QL // KV == 8
         and (KV * S) % 8 == 0
         and SPAN % 128 == 0
+        and NH * NA % 2 == 0
+        and NP * NH * NA * W == lm_head.shape[0]
+        and out_proj.shape[2] == NH * NA * W
         and W * VL * 2 * RING <= 60 * MIB
     )
     if not fits:

time: 48.1 us -> 43.1 us (0.90)
  Pallas kernels: 47.2 us -> 42.2 us
    pallas_call x1, Pallas kernels: 6.24 us -> 1.57 us  [one_kernel(): pl.pallas_call(closing, out_shape=(jax.ShapeDtypeStruct((R, VL), F32), ja...]
where the time goes in v4:
time: 43.1 us; the launch traced here: 42.8 us
  Pallas kernels  42.2 us (98%)
  between operations  0.64 us (1%)
    pallas_call x1, Pallas kernels, one_kernel(): pl.pallas_call(functools.partial(kernel, cfg), out_shape=(jax.ShapeDtypeS...  40.6 us
    pallas_call x1, Pallas kernels, one_kernel(): pl.pallas_call(closing, out_shape=(jax.ShapeDtypeStruct((R, VL), F32), ja...  1.57 us

profile of v4, /device:TPU:0, one launch (start us, length us, event | category | flops | bytes accessed | tf_op | source)
XLA Modules:
  0.0 42.8 jit_solution(16598154211523095468)
XLA Ops:
  0.6 40.6 %shard_map.122 = (f32[8,4096]{1,0:T(8,128)}, f32[1,8]{1,0:T(1,128)}) custom-call(s32[8]{0:T(128)} %slot_ref.1, s32[8]{0:T(128)} %len_ref.1, bf16[8,512]{1,0:T(8,128)(2,1)} %hidden_hbm.1, f32[1,512]{1,0:T(1,128)} %bitcast.2, bf16[2,4096]{1,0:T(2,128)(2,1)} %q_hbm.1, bf16[2,512]{1,0:T(2,128)(2,1)} %nk_hbm.1, bf16[2,512]{1,0:T(2,128)(2,1)} %nv_hbm.1, ...), custom_call_target="tpu_custom_call" | custom-call | flops 612368384 | bytes 76546048 | tf_op jit(solution)/shard_map/pallas_call | solution.py:449
  41.3 1.6 %shard_map.123 = (f32[8,4096]{1,0:T(8,128)}, f32[1,8]{1,0:T(1,128)}) custom-call(f32[8,4096]{1,0:T(8,128)} %get-tuple-element.6.logits_in, f32[1,8]{1,0:T(1,128)} %get-tuple-element.7.ent_in), custom_call_target="tpu_custom_call" | custom-call | tf_op jit(solution)/shard_map/pallas_call | solution.py:505

commit v5 on v4

--- a/solution.py
+++ b/solution.py
@@ -207,7 +207,7 @@
         for i, d in enumerate(quad)
     ]
     sent += h_copies
-    start_chunks(2, 4)
+    start_chunks(2, 5)
 
     slots = [slot_ref[r] for r in range(R)]
     lengths = [len_ref[r] for r in range(R)]
@@ -286,7 +286,7 @@
             send(send2.at[to["head"]], recv2.at[here], a_send.at[i], a_recv.at[i], to)
         )
     sent += a_copies
-    start_chunks(4, 6)
+    start_chunks(5, 9)
 
     RH = iota((HO * R, NP * B), 0)
     CH = iota((HO * R, NP * B), 1)
@@ -331,7 +331,7 @@
         for i, d in enumerate(quad)
     ]
     sent += t_copies
-    start_chunks(6, 8)
+    start_chunks(9, free)
     for c in h_copies:
         c.wait_recv()
     stream = two_rows([hidden_quad[n] for n in range(QUAD)])
@@ -344,7 +344,6 @@
     sent += [
         send(xs.at[p], xs.at[p], s_send.at[d], s_recv.at[p], at(d, 0, 0)) for d in range(1, NP)
     ]
-    start_chunks(8, free)
     for o in range(free, NBUF):
         lm_copy(o, o).start(priority=1)
 
@@ -379,20 +378,20 @@
             lefts.append((block * gains[q * QUAD + i]).astype(BF))
             squares = squares + jnp.sum(block * block, axis=1, keepdims=True)
         held = [lax.rem(g * QUAD + i, NBUF) for i in range(QUAD)]
-        for i in range(QUAD):
-            lm_copy(g * QUAD + i, held[i]).wait()
         part = VL // 4
-        for first in range(0, VL, part):
-            add = mm(lefts[0], ring[held[0], :, first : first + part])
-            for i in range(1, QUAD):
-                add = add + mm(lefts[i], ring[held[i], :, first : first + part])
-            acc[:, first : first + part] += add
-        for i in range(QUAD):
-            o = g * QUAD + i
-
-            @pl.when(o + NBUF < NCH)
-            def _():
-                lm_copy(o + NBUF, held[i]).start(priority=1)
+        for pair in range(0, QUAD, 2):
+            for i in (pair, pair + 1):
+                lm_copy(g * QUAD + i, held[i]).wait()
+            for first in range(0, VL, part):
+                add = mm(lefts[pair], ring[held[pair], :, first : first + part])
+                add = add + mm(lefts[pair + 1], ring[held[pair + 1], :, first : first + part])
+                acc[:, first : first + part] += add
+            for i in (pair, pair + 1):
+                o = g * QUAD + i
+
+                @pl.when(o + NBUF < NCH)
+                def _():
+                    lm_copy(o + NBUF, held[i]).start(priority=1)
 
         return squares
 

time: 43.1 us -> 41.2 us (0.956)
  Pallas kernels: 42.2 us -> 40.3 us
    pallas_call x1, Pallas kernels: 40.6 us -> 38.8 us  [one_kernel(): pl.pallas_call(functools.partial(kernel, cfg), out_shape=(jax.ShapeDtypeS...]
where the time goes in v5:
time: 41.2 us; the launch traced here: 41 us
  Pallas kernels  40.3 us (98%)
  between operations  0.64 us (2%)
    pallas_call x1, Pallas kernels, one_kernel(): pl.pallas_call(functools.partial(kernel, cfg), out_shape=(jax.ShapeDtypeS...  38.8 us
    pallas_call x1, Pallas kernels, one_kernel(): pl.pallas_call(closing, out_shape=(jax.ShapeDtypeStruct((R, VL), F32), ja...  1.57 us

profile of v5, /device:TPU:0, one launch (start us, length us, event | category | flops | bytes accessed | tf_op | source)
XLA Modules:
  0.0 41.0 jit_solution(1486693949903654067)
XLA Ops:
  0.6 38.8 %shard_map.122 = (f32[8,4096]{1,0:T(8,128)}, f32[1,8]{1,0:T(1,128)}) custom-call(s32[8]{0:T(128)} %slot_ref.1, s32[8]{0:T(128)} %len_ref.1, bf16[8,512]{1,0:T(8,128)(2,1)} %hidden_hbm.1, f32[1,512]{1,0:T(1,128)} %bitcast.2, bf16[2,4096]{1,0:T(2,128)(2,1)} %q_hbm.1, bf16[2,512]{1,0:T(2,128)(2,1)} %nk_hbm.1, bf16[2,512]{1,0:T(2,128)(2,1)} %nv_hbm.1, ...), custom_call_target="tpu_custom_call" | custom-call | flops 612368384 | bytes 76546048 | tf_op jit(solution)/shard_map/pallas_call | solution.py:448
  39.4 1.6 %shard_map.123 = (f32[8,4096]{1,0:T(8,128)}, f32[1,8]{1,0:T(1,128)}) custom-call(f32[8,4096]{1,0:T(8,128)} %get-tuple-element.6.logits_in, f32[1,8]{1,0:T(1,128)} %get-tuple-element.7.ent_in), custom_call_target="tpu_custom_call" | custom-call | tf_op jit(solution)/shard_map/pallas_call | solution.py:504
